TPU v7x, 32 devices: a whole 2x2x4 slice. The times are simulated.
32 devices in a mesh: groups: 2 (over y), dp: 8 (over z, x), tensor: 2 (over core).
Axes of the slice: x: 2, y: 2, z: 4, core: 2. Of those that a mesh axis runs over, the one named last changes fastest.
Arguments:
- inputs: bfloat16 [2048, 8192], P(('groups', 'dp'), 'tensor'), parts along dimension 0, may hold values from -6 to 6
- output_gradient: bfloat16 [2048, 4096], P(('groups', 'dp')), parts along dimension 0, may hold values from -6 to 6
- frozen_output: bfloat16 [2048, 4096], P(('groups', 'dp')), parts along dimension 0, may hold values from -6 to 6
- tenant_of_tile: int32 [32], P(('groups', 'dp')), parts along dimension 0, may hold values from 0 to 7, as said below
- frozen_weight: bfloat16 [4096, 8192], P('dp', 'tensor'), may hold values from -1 to 1
- adapter_down: bfloat16 [8, 16, 8192], P(None, None, 'tensor'), may hold values from -2 to 2
- adapter_up: bfloat16 [8, 4096, 16], P(None, 'dp'), may hold values from -1.5 to 1.5
- magnitude: float32 [8, 4096], P(None, 'dp'), may hold values from 0.5 to 2
Outputs:
- grad_up: float32 [16, 4096, 16], P('groups', ('dp', 'tensor')), parts along dimension 0
- grad_mag: float32 [16, 4096], P('groups', ('dp', 'tensor')), parts along dimension 0
- grad_down: float32 [256, 8192], P(('groups', 'dp'), 'tensor'), parts along dimension 0
There are 2 independent parts, one for each index of `groups`. A program takes and returns all parts, laid end to end along the dimension named above; an argument that names none is the same for every part. Nothing has to cross between parts.
Inputs may be any that keep to these rules, and one draw needn't show every extreme that they name: `tenant_of_tile`: within the 2 tiles of each index of dp the tenants do not decrease; every tenant owns at least one tile.
All inputs are finite; a program needn't handle non-finite values.
Results may differ from a plain program's by a relative error of at most 0.0037.
The roundings to bfloat16 on the way count: a program that leaves them out, or rounds other values in their place, can miss the bound.
Values may be sent and summed in bfloat16 or wider, within the bound.
A program may use at most 64 MiB of HBM per device.

v0:
```python
import jax
import jax.numpy as jnp
from jax import lax
from jax.sharding import PartitionSpec as P


def local(
    inputs,
    output_gradient,
    frozen_output,
    tenant_of_tile,
    frozen_weight,
    adapter_down,
    adapter_up,
    magnitude,
):
    hi = lax.Precision.HIGHEST
    tenant_list, rank_dimension, input_local = adapter_down.shape
    own_rows = frozen_weight.shape[0]
    token_rows = inputs.shape[0]
    tile_count = tenant_of_tile.shape[0]
    tile_len = token_rows // tile_count
    tensor_count = lax.axis_size("tensor")
    data_count = lax.axis_size("dp")
    row_halves_split = own_rows // tensor_count
    span_cols = data_count * row_halves_split
    shifted_values = jnp.einsum(
        "sxh,shj->sxj", adapter_up, adapter_down, preferred_element_type=jnp.float32
    )
    merged = frozen_weight.astype(jnp.float32)[None] + shifted_values
    partial_sq = jnp.sum(merged * merged, axis=2)
    tile_onehot = (
        tenant_of_tile[:, None] == jnp.arange(tenant_list, dtype=jnp.int32)[None, :]
    ).astype(jnp.float32)
    row_tenant = jnp.repeat(jnp.arange(tenant_list, dtype=jnp.int32), rank_dimension)
    row_rank = jnp.tile(jnp.arange(rank_dimension, dtype=jnp.int32), tenant_list)
    col_tenant = jnp.repeat(tenant_of_tile, rank_dimension)
    col_rank = jnp.tile(jnp.arange(rank_dimension, dtype=jnp.int32), tile_count)
    placement = (
        (row_tenant[:, None] == col_tenant[None, :]) & (row_rank[:, None] == col_rank[None, :])
    ).astype(jnp.float32)
    tile_inputs = inputs.reshape(tile_count, tile_len, input_local)
    selected_down = jnp.take(adapter_down, tenant_of_tile, axis=0)
    rank_part = jnp.einsum(
        "tsi,tri->tsr", tile_inputs, selected_down, preferred_element_type=jnp.float32
    )
    norm_sq = lax.psum(partial_sq, "tensor")
    rank_sum = lax.psum(rank_part, "tensor")
    norm_values = jnp.sqrt(norm_sq)
    tile_position = lax.axis_index("tensor") * row_halves_split
    scale_own = lax.dynamic_slice_in_dim(
        magnitude / norm_values, tile_position, row_halves_split, 1
    )
    norm_own = lax.dynamic_slice_in_dim(norm_values, tile_position, row_halves_split, 1)
    owned_up_rows = lax.dynamic_slice_in_dim(adapter_up, tile_position, row_halves_split, 1)
    scales = lax.all_gather(scale_own, "dp", axis=1, tiled=True)
    up_cols = lax.all_gather(owned_up_rows, "dp", axis=1, tiled=True)

    def select_cols(full):
        shaped = full.reshape(token_rows, data_count, tensor_count, row_halves_split)
        picked = lax.dynamic_index_in_dim(shaped, lax.axis_index("tensor"), 2, keepdims=False)
        return picked.reshape(tile_count, tile_len, span_cols)

    grad_cols = select_cols(output_gradient)
    base_cols = select_cols(frozen_output)
    rank_low = rank_sum.astype(jnp.bfloat16)
    up_sel = jnp.take(up_cols, tenant_of_tile, axis=0)
    scale_sel = jnp.take(scales, tenant_of_tile, axis=0)
    mixed_out = base_cols.astype(jnp.float32) + jnp.einsum(
        "tsr,tor->tso", rank_low, up_sel, preferred_element_type=jnp.float32
    )
    grad_f = grad_cols.astype(jnp.float32)
    tile_mag = jnp.sum(grad_f * mixed_out, axis=1)
    mag_part = jnp.dot(tile_onehot.T, tile_mag, precision=hi)
    scaled_grad = (grad_f * scale_sel[:, None, :]).astype(jnp.bfloat16)
    up_tile = jnp.einsum("tsr,tso->tro", rank_low, scaled_grad, preferred_element_type=jnp.float32)
    up_part = jnp.dot(
        placement, up_tile.reshape(tile_count * rank_dimension, span_cols), precision=hi
    )
    back_part = jnp.einsum("tso,tor->tsr", scaled_grad, up_sel, preferred_element_type=jnp.float32)
    back_sum = lax.psum(back_part, "tensor")
    back_low = back_sum.astype(jnp.bfloat16)
    down_tile = jnp.einsum(
        "tsr,tsi->tri", back_low, tile_inputs, preferred_element_type=jnp.float32
    ).reshape(tile_count * rank_dimension, input_local)
    up_sum = lax.psum_scatter(up_part, "dp", scatter_dimension=1, tiled=True)
    mag_sum = lax.psum_scatter(mag_part, "dp", scatter_dimension=1, tiled=True)
    grad_mag = mag_sum / norm_own
    grad_up = jnp.transpose(
        up_sum.reshape(tenant_list, rank_dimension, row_halves_split), (0, 2, 1)
    )
    down_part = jnp.dot(placement, down_tile, precision=hi)
    grad_down = lax.psum_scatter(down_part, "dp", scatter_dimension=0, tiled=True)
    return (grad_up, grad_mag, grad_down)


def solution(mesh):
    placed = (
        P(("groups", "dp"), "tensor"),
        P(("groups", "dp"), None),
        P(("groups", "dp"), None),
        P(("groups", "dp")),
        P("dp", "tensor"),
        P(None, None, "tensor"),
        P(None, "dp", None),
        P(None, "dp"),
    )
    return jax.shard_map(
        local,
        mesh=mesh,
        in_specs=placed,
        out_specs=(
            P("groups", ("dp", "tensor"), None),
            P("groups", ("dp", "tensor")),
            P(("groups", "dp"), "tensor"),
        ),
        check_vma=False,
    )
```

profile of v0, /device:TPU:0, one launch (start us, length us, event | category | flops | bytes accessed | tf_op | source)
XLA Modules:
  0.0 321.3 jit_solution(2901252112926799213)
XLA Ops:
  7.2 0.0 copy-start
  7.2 0.0 copy-start.1
  7.2 0.0 copy-start.3
  7.2 0.0 reduce-scatter.6.cloned.1.call-start
  7.2 0.8 compare_select_fusion
  8.1 1.2 compare_and_fusion.3
  9.2 3.3 %convert_element_type.29 = f32[512,4096]{1,0:T(8,128)S(1)} convert(bf16[512,4096]{1,0:T(8,128)(2,1)} %param.12) | non-fusion elementwise | flops 2097152 | bytes 12582912 | tf_op jit(solution)/shard_map/convert_element_type | solution.py:30
  12.5 0.0 copy-done.1
  12.5 0.0 copy-done.3
  12.5 0.0 copy-start.5
  12.5 0.0 copy-start.2
  12.5 9.8 %multiply_reduce_fusion = f32[8,512]{1,0:T(8,128)S(1)} fusion(bf16[8,512,16]{1,2,0:T(8,128)(2,1)S(1)} %copy-done.3, bf16[8,16,4096]{2,1,0:T(8,128)(2,1)S(1)} %copy-done.1, f32[512,4096]{1,0:T(8,128)S(1)} %convert_element_type.29), kind=kOutput, calls=%fused_computation.3 | convolution fusion | flops 587198464 | bytes 9584640 | tf_op jit(solution)/shard_map/sxh,shj->sxj/dot_general | solution.py:27
  22.3 3.6 %psum.22 = f32[8,512]{1,0:T(8,128)S(1)} all-reduce(f32[8,512]{1,0:T(8,128)S(1)} %multiply_reduce_fusion), channel_id=1, replica_groups=mesh['groups'=2,'dp'=8,'tensor'=2] {'tensor'}, use_global_device_ids=true, to_apply=%region_2.3 | all-reduce | flops 4096 | bytes 32768 | tf_op jit(solution)/shard_map/psum | solution.py:47
  25.9 0.0 copy-start.4
  26.0 0.6 constant_dynamic-slice_fusion
  26.6 0.0 copy-done.5
  26.6 32.0 %all_gather.6 = f32[8,2048]{1,0:T(8,128)S(1)} all-gather(f32[8,256]{1,0:T(8,128)S(1)} %dynamic-slice_divide_fusion), channel_id=1, replica_groups=mesh['groups'=2,'dp'=8,'tensor'=2] {'dp'}, dimensions={1}, use_global_device_ids=true | all-gather | bytes 73728 | tf_op jit(solution)/shard_map/all_gather | solution.py:56
  58.6 0.0 copy-done.4
  58.6 0.6 gather_fusion
  59.2 1.2 gather_fusion.1
  60.4 31.6 %all_gather.7 = bf16[8,2048,16]{1,2,0:T(8,128)(2,1)S(1)} all-gather(bf16[8,256,16]{1,2,0:T(8,128)(2,1)} %constant_dynamic-slice_fusion), channel_id=1, replica_groups=mesh['groups'=2,'dp'=8,'tensor'=2] {'dp'}, dimensions={1}, use_global_device_ids=true | all-gather | bytes 589824 | tf_op jit(solution)/shard_map/all_gather | solution.py:57
  91.9 0.6 gather_fusion.2
  92.5 0.0 copy-done.2
  92.5 0.8 reshape.56
  93.3 3.0 convert_reduce_fusion.1
  96.3 0.2 reshape.61
  96.5 1.8 reshape.59
  98.4 4.0 %convert_reduce_fusion = f32[128,8,256]{2,1,0:T(8,128)} fusion(bf16[128,8,2,256]{3,2,1,0:T(2,128)(2,1)S(1)} %reshape.59, s32[]{:T(128)S(6)} %select_n.37), kind=kLoop, calls=%fused_computation.8 | loop fusion | flops 262144 | bytes 1572868 | tf_op jit(solution)/shard_map/convert_element_type | solution.py:69
  102.4 1.4 reshape.62
  103.8 0.8 broadcast_select_fusion.3
  104.5 0.0 copy-done
  104.6 1.7 convolution_bitcast_fusion
  106.3 1.0 fusion.4
  107.2 4.0 %all-reduce = (bf16[2,64,16]{1,2,0:T(8,128)(2,1)S(1)}, bf16[2,64,16]{1,2,0:T(8,128)(2,1)S(1)}) all-reduce(f32[2,64,16]{1,2,0:T(8,128)} %convolution_bitcast_fusion, f32[2,64,16]{1,2,0:T(8,128)S(1)} %fusion.4), channel_id=1, replica_groups=mesh['groups'=2,'dp'=8,'tensor'=2] {'tensor'}, use_global_device_ids=true, to_apply=%region_0.0 | all-reduce | flops 4096 | bytes 24576 | tf_op jit(solution)/shard_map/psum | solution.py:48
  111.3 1.0 fusion.1
  112.3 1.6 fusion.21
  113.9 0.0 reduce-scatter.6.cloned.1.call-update
  113.9 0.0 reduce-scatter.4.cloned.1.call-start
  113.9 0.2 fusion.5
  114.1 0.1 eq.47
  114.2 0.1 eq.52
  114.3 0.7 broadcast_in_dim.43
  115.0 0.1 eq.49
  115.1 0.1 eq.54
  115.2 1.6 fusion.8
  116.8 0.0 reduce-scatter.4.cloned.1.call-update
  116.8 0.0 reduce-scatter.8.cloned.1.call-start
  116.9 0.3 fusion.28
  117.1 2.4 fusion.7
  119.5 0.0 reduce-scatter.8.cloned.1.call-update
  119.5 56.8 %reduce-scatter.6.cloned.1.call-done = f32[8,256]{1,0:T(8,128)} async-done(((f32[8,2048]{1,0:T(8,128)}), f32[8,256]{1,0:T(8,128)}) %reduce-scatter.6.cloned.1.call-update) | async-done | bytes 8208 | tf_op jit(solution)/shard_map/reduce_scatter | solution.py:87
  176.4 1.3 dynamic-slice_divide_fusion.1
  177.7 65.6 %reduce-scatter.4.cloned.1.call-done = f32[128,256]{1,0:T(8,128)} async-done(((f32[128,2048]{1,0:T(8,128)}), f32[128,256]{1,0:T(8,128)}) %reduce-scatter.4.cloned.1.call-update) | async-done | bytes 131088 | tf_op jit(solution)/shard_map/reduce_scatter | solution.py:86
  243.2 71.5 %reduce-scatter.8.cloned.1.call-done = f32[16,4096]{1,0:T(8,128)} async-done(((f32[128,4096]{1,0:T(8,128)}), f32[16,4096]{1,0:T(8,128)}) %reduce-scatter.8.cloned.1.call-update) | async-done | bytes 262160 | tf_op jit(solution)/shard_map/reduce_scatter | solution.py:93
  (6 shorter events, 0.0 us)
Async XLA Ops:
  7.2 97.4 %copy-start = (bf16[128,4096]{1,0:T(8,128)(2,1)S(1)}, bf16[128,4096]{1,0:T(8,128)(2,1)}, u32[]{:S(2)}) copy-start(bf16[128,4096]{1,0:T(8,128)(2,1)} %param.8) | copy-start | bytes 3145732
  7.2 5.3 %copy-start.1 = (bf16[8,16,4096]{2,1,0:T(8,128)(2,1)S(1)}, bf16[8,16,4096]{2,1,0:T(8,128)(2,1)}, u32[]{:S(2)}) copy-start(bf16[8,16,4096]{2,1,0:T(8,128)(2,1)} %param.13) | copy-start | bytes 3145732
  7.2 5.3 %copy-start.3 = (bf16[8,512,16]{1,2,0:T(8,128)(2,1)S(1)}, bf16[8,512,16]{1,2,0:T(8,128)(2,1)}, u32[]{:S(2)}) copy-start(bf16[8,512,16]{1,2,0:T(8,128)(2,1)} %param.14) | copy-start | bytes 393220
  7.2 169.2 %reduce-scatter.6.cloned.1.call-start = ((), (), s32[]{:S(2)}) async-start(), calls=%async_computation.4 | async-start | bytes 73728 | tf_op jit(solution)/shard_map/reduce_scatter | solution.py:87
  12.5 14.1 %copy-start.5 = (f32[8,512]{1,0:T(8,128)S(1)}, f32[8,512]{1,0:T(8,128)}, u32[]{:S(2)}) copy-start(f32[8,512]{1,0:T(8,128)} %param.15) | copy-start | bytes 49156
  12.5 80.0 %copy-start.2 = (bf16[128,4096]{1,0:T(8,128)(2,1)S(1)}, bf16[128,4096]{1,0:T(8,128)(2,1)}, u32[]{:S(2)}) copy-start(bf16[128,4096]{1,0:T(8,128)(2,1)} %param.9) | copy-start | bytes 3145732
  25.9 32.7 %copy-start.4 = (f32[8,512]{1,0:T(8,128)}, f32[8,512]{1,0:T(8,128)S(1)}, u32[]{:S(2)}) copy-start(f32[8,512]{1,0:T(8,128)S(1)} %sqrt.3) | copy-start | bytes 49156
  113.9 129.4 %reduce-scatter.4.cloned.1.call-start = ((), (), s32[]{:S(2)}) async-start(), calls=%async_computation.3 | async-start | bytes 1179648 | tf_op jit(solution)/shard_map/reduce_scatter | solution.py:86
  116.8 198.0 %reduce-scatter.8.cloned.1.call-start = ((), (), s32[]{:S(2)}) async-start(), calls=%async_computation.5 | async-start | bytes 2359296 | tf_op jit(solution)/shard_map/reduce_scatter | solution.py:93
Sparse Core Ops, SparseCore 0:
  114.0 62.3 reduce-scatter.5
  180.3 62.8 reduce-scatter.3
  247.8 66.9 reduce-scatter.7
where the time goes:
time: 322 us; the launch traced here: 321 us
  waiting for transfers between devices  194 us (60%)
  blocking collectives  71.3 us (22%)
  matrix products  19.4 us (6%)
  other arithmetic  14.4 us (4%)
  between operations  13.9 us (4%)
  local copies, waits for them, and re-layouts  8.22 us (3%)
    reduce_scatter x1, waiting for transfers between devices, local(): lax.psum_scatter(down_part, 'dp', scatter_dimension=0, tiled=True)  71.5 us
    reduce_scatter x1, waiting for transfers between devices, local(): up_sum = lax.psum_scatter(up_part, 'dp', scatter_dimension=1, tiled=True)  65.6 us
    reduce_scatter x1, waiting for transfers between devices, local(): mag_sum = lax.psum_scatter(mag_part, 'dp', scatter_dimension=1, tiled=True)  56.8 us
    all_gather x1, blocking collectives, local(): scales = lax.all_gather(scale_own, 'dp', axis=1, tiled=True)  32 us
    all_gather x1, blocking collectives, local(): up_cols = lax.all_gather(owned_up_rows, 'dp', axis=1, tiled=True)  31.6 us
    dot_general x1, matrix products, local(): jnp.einsum('sxh,shj->sxj', adapter_up, adapter_down, preferred_element_ty...  9.75 us
  transfers between devices with their start and end apart: 3, of which 3 were waited for; matrix products, arithmetic and copies ran while one was open for 2% of the time, Pallas kernels for 0%

commit v1 on v0

--- a/solution.py
+++ b/solution.py
@@ -1,10 +1,14 @@
+import functools
+
 import jax
 import jax.numpy as jnp
 from jax import lax
+from jax.experimental import pallas as pl
+from jax.experimental.pallas import tpu as pltpu
 from jax.sharding import PartitionSpec as P
 
 
-def local(
+def plain(
     inputs,
     output_gradient,
     frozen_output,
@@ -94,6 +98,329 @@
     return (grad_up, grad_mag, grad_down)
 
 
+F32 = jnp.float32
+BF16 = jnp.bfloat16
+NT = (((1,), (1,)), ((), ()))
+
+
+def iota(shape, dim):
+    return lax.broadcasted_iota(jnp.int32, shape, dim)
+
+
+def exchange_kernel(
+    N, T, K, R,
+    ten_ref, x_ref, g_ref, f_ref, down_ref, up_ref, mag_ref, sq_ref,
+    up_out, mag_out, down_out,
+    g_buf, aux_send, aux_buf, sq_buf, rp_send, rp_buf, ra_buf, up_acc, z_acc, fg_acc,
+    back_send, back_buf, tile_send, tile_buf, part_send, part_buf,
+    g_ss, g_rs, aux_ss, aux_rs, pair_ss, pair_rs, ra_ss, ra_rs,
+    back_ss, back_rs, tile_ss, tile_rs, part_ss, part_rs,
+):
+    me = lax.axis_index("dp")
+    core = lax.axis_index("tensor")
+    other = 1 - core
+    tok = x_ref.shape[0]
+    half = tok // 2
+    width = x_ref.shape[1] // N
+    C = up_ref.shape[1]
+    KR = K * R
+
+    def copy(src, dst, ss, rs, dp, tensor):
+        return pltpu.make_async_remote_copy(
+            src_ref=src, dst_ref=dst, send_sem=ss, recv_sem=rs,
+            device_id={"dp": dp, "tensor": tensor}, device_id_type=pl.DeviceIdType.MESH,
+        )
+
+    def peer(off):
+        return lax.rem(me + off, N)
+
+    barrier = pltpu.get_barrier_semaphore()
+    for off in range(N):
+        for t in ((other,) if off == 0 else (core, other)):
+            pl.semaphore_signal(
+                barrier, inc=1, device_id={"dp": peer(off), "tensor": t},
+                device_id_type=pl.DeviceIdType.MESH,
+            )
+    pl.semaphore_wait(barrier, 2 * N - 1)
+
+    def cols(d):
+        return pl.ds(pl.multiple_of((d * T + core) * C, C), C)
+
+    def span(d):
+        return pl.ds(pl.multiple_of(d * width, width), width)
+
+    def g_copy(d):
+        return copy(g_ref.at[:, cols(d)], g_buf.at[me], g_ss.at[d], g_rs.at[me], d, core)
+
+    def aux_copy(d):
+        return copy(aux_send.at[d], aux_buf.at[me], aux_ss.at[d], aux_rs.at[me], d, core)
+
+    sq_copy = copy(
+        sq_ref.at[:, pl.ds(pl.multiple_of(other * C, C), C)], sq_buf,
+        pair_ss.at[0], pair_rs.at[0], me, other,
+    )
+    sq_copy.start()
+
+    def start_g(off, _):
+        g_copy(peer(off)).start()
+        return 0
+    lax.fori_loop(1, N, start_g, 0)
+
+    ten0 = ten_ref[0]
+    ten1 = ten_ref[1]
+    lane_tok = iota((1, tok), 1)
+    own_ten = jnp.where(lane_tok < half, ten0, ten1)
+    own_mask = (iota((KR, tok), 0) // R) == own_ten
+
+    proj = lax.dot_general(down_ref[...], x_ref[...], NT, preferred_element_type=F32)
+    rp_send[...] = jnp.sum(jnp.where(own_mask, proj, 0.0).reshape(K, R, tok), axis=0)
+    rp_copy = copy(rp_send, rp_buf, pair_ss.at[1], pair_rs.at[1], me, other)
+    rp_copy.start()
+
+    lane = iota((1, C), 1)
+    rows = iota((8, C), 0)
+    ids0 = jnp.full((1, C), ten0, jnp.int32)
+    ids1 = jnp.full((1, C), ten1, jnp.int32)
+    tok_ids = jnp.where(lax.rem(lane, tok) < half, ten0, ten1)
+    slot_ids = jnp.where(lane // (2 * R) == me, jnp.where(lax.rem(lane, 2 * R) < R, ten0, ten1), 0)
+    ids = jnp.where(rows == 2, ids0, jnp.where(rows == 3, ids1, jnp.where(rows == 4, tok_ids, slot_ids)))
+    ids = jnp.where((rows >= 2) & (rows <= 5), ids, 0).astype(F32)
+
+    def make_aux(off, _):
+        d = peer(off)
+        prod = g_ref[:, cols(d)].astype(F32) * f_ref[:, cols(d)].astype(F32)
+        s0 = jnp.sum(prod[:half], axis=0, keepdims=True)
+        s1 = jnp.sum(prod[half:], axis=0, keepdims=True)
+        aux_send[d] = jnp.where(rows == 0, s0, jnp.where(rows == 1, s1, ids))
+        return 0
+
+    def start_aux(off, _):
+        make_aux(off, 0)
+        aux_copy(peer(off)).start()
+        return 0
+    lax.fori_loop(1, N, start_aux, 0)
+    make_aux(0, 0)
+    aux_buf[me] = aux_send[me]
+    g_buf[me] = g_ref[:, cols(me)]
+
+    rp_copy.wait_recv()
+    a = rp_send[...]
+    b = rp_buf[...]
+    ra_buf[me] = (a + b).astype(BF16)
+
+    def ra_copy(d):
+        return copy(ra_buf.at[me], ra_buf.at[me], ra_ss.at[d], ra_rs.at[me], d, core)
+
+    def start_ra(off, _):
+        ra_copy(peer(off)).start()
+        return 0
+    lax.fori_loop(1, N, start_ra, 0)
+
+    sq_copy.wait_recv()
+    norm = jnp.sqrt(sq_ref[:, pl.ds(pl.multiple_of(core * C, C), C)] + sq_buf[...])
+    scale = mag_ref[...] / norm
+    up = up_ref[...]
+
+    up_acc[...] = jnp.zeros_like(up_acc)
+    z_acc[...] = jnp.zeros_like(z_acc)
+    fg_acc[...] = jnp.zeros_like(fg_acc)
+
+    def owner_block(s):
+        aux = aux_buf[s]
+        fg = fg_acc[...]
+        sel0 = jnp.zeros((1, C), F32)
+        sel1 = jnp.zeros((1, C), F32)
+        krow = iota((K, C), 0).astype(F32)
+        hit0 = krow == aux[2:3]
+        hit1 = krow == aux[3:4]
+        fg_acc[...] = fg + jnp.where(hit0, aux[0:1], 0.0) + jnp.where(hit1, aux[1:2], 0.0)
+        sel0 = jnp.sum(jnp.where(hit0, scale, 0.0), axis=0, keepdims=True)
+        sel1 = jnp.sum(jnp.where(hit1, scale, 0.0), axis=0, keepdims=True)
+        g = g_buf[s]
+        gf = g.astype(F32)
+        scaled = (gf * jnp.where(iota((tok, C), 0) < half, sel0, sel1)).astype(BF16)
+        mask = (iota((KR, tok), 0) // R).astype(F32) == aux[4:5, :tok]
+        ra = ra_buf[s].astype(F32)
+        wide = jnp.where(mask, jnp.concatenate([ra] * K, axis=0), 0.0).astype(BF16)
+        up_acc[...] += jnp.dot(wide, scaled, preferred_element_type=F32)
+        z_acc[...] += jnp.dot(wide, g, preferred_element_type=F32)
+        back = lax.dot_general(up, scaled, NT, preferred_element_type=F32)
+        return jnp.sum(jnp.where(mask, back, 0.0).reshape(K, R, tok), axis=0)
+
+    mine = me * T + core
+
+    def back_copy(s, t):
+        return copy(
+            back_send.at[s], back_buf.at[mine], back_ss.at[s * T + t], back_rs.at[mine], s, t
+        )
+
+    own_back = owner_block(me)
+    back_send[me] = own_back
+    back_copy(me, other).start()
+    back_buf[mine] = own_back
+
+    def remote_block(off, _):
+        s = peer(off)
+        copy(aux_send.at[s], aux_buf.at[s], aux_ss.at[s], aux_rs.at[s], s, core).wait_recv()
+        copy(ra_buf.at[s], ra_buf.at[s], ra_ss.at[s], ra_rs.at[s], s, core).wait_recv()
+        copy(g_buf.at[s], g_buf.at[s], g_ss.at[s], g_rs.at[s], s, core).wait_recv()
+        back_send[s] = owner_block(s)
+        back_copy(s, core).start()
+        back_copy(s, other).start()
+        return 0
+    lax.fori_loop(1, N, remote_block, 0)
+
+    up_sum = up_acc[...]
+    up_out[...] = up_sum
+    mixed = jnp.sum((up.astype(F32) * z_acc[...]).reshape(K, R, C), axis=1)
+    mag_out[...] = (fg_acc[...] + mixed) / norm
+
+    def wait_back(s, t):
+        i = s * T + t
+        copy(back_send.at[s], back_buf.at[i], back_ss.at[i], back_rs.at[i], s, t).wait_recv()
+
+    def wait_backs(off, _):
+        wait_back(peer(off), core)
+        wait_back(peer(off), other)
+        return 0
+    wait_back(me, other)
+    lax.fori_loop(1, N, wait_backs, 0)
+    rank_grad = jnp.sum(back_buf[...], axis=0).astype(BF16).astype(F32)
+    two = jnp.concatenate([rank_grad, rank_grad], axis=0)
+    lhs = jnp.where((iota((2 * R, tok), 0) // R) == (iota((2 * R, tok), 1) // half), two, 0.0).astype(BF16)
+
+    def tile_copy(d):
+        return copy(tile_send.at[d], tile_buf.at[me], tile_ss.at[d], tile_rs.at[me], d, core)
+
+    def start_tile(off, _):
+        d = peer(off)
+        tile_send[d] = jnp.dot(lhs, x_ref[:, span(d)], preferred_element_type=F32).astype(BF16)
+        tile_copy(d).start()
+        return 0
+    lax.fori_loop(1, N, start_tile, 0)
+    tile_buf[me] = jnp.dot(lhs, x_ref[:, span(me)], preferred_element_type=F32).astype(BF16)
+
+    slot_ten = jnp.sum(aux_buf[:, 5, :], axis=0, keepdims=True)
+    prow = iota((KR, C), 0)
+    place = ((prow // R).astype(F32) == slot_ten) & (lax.rem(prow, R) == lax.rem(iota((KR, C), 1), R))
+    place = jnp.where(place, 1.0, 0.0).astype(BF16)
+
+    def wait_tile(off, _):
+        s = peer(off)
+        copy(tile_send.at[s], tile_buf.at[s], tile_ss.at[s], tile_rs.at[s], s, core).wait_recv()
+        return 0
+    lax.fori_loop(1, N, wait_tile, 0)
+    part = jnp.dot(place, tile_buf[...].reshape(N * 2 * R, width), preferred_element_type=F32)
+    part_send[...] = part.astype(BF16).reshape(N, R, width)
+
+    def part_copy(d):
+        return copy(part_send.at[d], part_buf.at[me], part_ss.at[d], part_rs.at[me], d, core)
+
+    def start_part(off, _):
+        part_copy(peer(off)).start()
+        return 0
+    lax.fori_loop(1, N, start_part, 0)
+    part_buf[me] = part_send[me]
+
+    def wait_sends(off, _):
+        d = peer(off)
+        g_copy(d).wait_send()
+        aux_copy(d).wait_send()
+        ra_copy(d).wait_send()
+        back_copy(d, core).wait_send()
+        back_copy(d, other).wait_send()
+        tile_copy(d).wait_send()
+        return 0
+    sq_copy.wait_send()
+    rp_copy.wait_send()
+    back_copy(me, other).wait_send()
+    lax.fori_loop(1, N, wait_sends, 0)
+
+    down_out[:, span(me)] = part_buf[me].astype(F32)
+
+    def finish(off, _):
+        s = peer(off)
+        copy(part_send.at[s], part_buf.at[s], part_ss.at[s], part_rs.at[s], s, core).wait_recv()
+        down_out[:, span(s)] = part_buf[s].astype(F32)
+        part_copy(s).wait_send()
+        return 0
+    lax.fori_loop(1, N, finish, 0)
+
+
+def exchange(ten, x, g, f, down, up, mag, sq, N, T, K, R):
+    tok, I = x.shape
+    C = up.shape[1]
+    width = I // N
+    vm = pltpu.VMEM
+    dma = pltpu.SemaphoreType.DMA
+    spec = pl.BlockSpec(memory_space=pltpu.VMEM)
+    return pl.pallas_call(
+        functools.partial(exchange_kernel, N, T, K, R),
+        out_shape=(
+            jax.ShapeDtypeStruct((K * R, C), F32),
+            jax.ShapeDtypeStruct((K, C), F32),
+            jax.ShapeDtypeStruct((R, I), F32),
+        ),
+        in_specs=[pl.BlockSpec(memory_space=pltpu.SMEM)] + [spec] * 7,
+        out_specs=(spec, spec, spec),
+        scratch_shapes=[
+            vm((N, tok, C), BF16), vm((N, 8, C), F32), vm((N, 8, C), F32), vm((K, C), F32),
+            vm((R, tok), F32), vm((R, tok), F32), vm((N, R, tok), BF16),
+            vm((K * R, C), F32), vm((K * R, C), F32), vm((K, C), F32),
+            vm((N, R, tok), F32), vm((N * T, R, tok), F32),
+            vm((N, 2 * R, width), BF16), vm((N, 2 * R, width), BF16),
+            vm((N, R, width), BF16), vm((N, R, width), BF16),
+            dma((N,)), dma((N,)), dma((N,)), dma((N,)), dma((2,)), dma((2,)),
+            dma((N,)), dma((N,)), dma((N * T,)), dma((N * T,)),
+            dma((N,)), dma((N,)), dma((N,)), dma((N,)),
+        ],
+        compiler_params=pltpu.CompilerParams(
+            collective_id=0, has_side_effects=True, vmem_limit_bytes=40 * 1024 * 1024
+        ),
+    )(ten, x, g, f, down, up, mag, sq)
+
+
+def partial_norms(weight, down, up):
+    shifted = jnp.einsum("sxh,shj->sxj", up, down, preferred_element_type=F32)
+    merged = weight.astype(F32)[None] + shifted
+    return jnp.sum(merged * merged, axis=2)
+
+
+def local(
+    inputs,
+    output_gradient,
+    frozen_output,
+    tenant_of_tile,
+    frozen_weight,
+    adapter_down,
+    adapter_up,
+    magnitude,
+):
+    K, R, I = adapter_down.shape
+    N = lax.axis_size("dp")
+    T = lax.axis_size("tensor")
+    own = frozen_weight.shape[0]
+    C = own // T
+    if not (
+        N == K and T == 2 and R == 16 and K == 8 and C == N * 2 * R
+        and inputs.shape[0] == 128 and tenant_of_tile.shape[0] == 2 and I % (128 * N) == 0
+    ):
+        return plain(
+            inputs, output_gradient, frozen_output, tenant_of_tile,
+            frozen_weight, adapter_down, adapter_up, magnitude,
+        )
+    sq = partial_norms(frozen_weight, adapter_down, adapter_up)
+    at = lax.axis_index("tensor") * C
+    up = jnp.transpose(lax.dynamic_slice_in_dim(adapter_up, at, C, 1), (0, 2, 1)).reshape(K * R, C)
+    mag = lax.dynamic_slice_in_dim(magnitude, at, C, 1)
+    up_sum, grad_mag, grad_down = exchange(
+        tenant_of_tile, inputs, output_gradient, frozen_output,
+        adapter_down.reshape(K * R, I), up, mag, sq, N, T, K, R,
+    )
+    grad_up = jnp.transpose(up_sum.reshape(K, R, C), (0, 2, 1))
+    return (grad_up, grad_mag, grad_down)
+
+
 def solution(mesh):
     placed = (
         P(("groups", "dp"), "tensor"),

time: 322 us -> 56.6 us (0.18)
  waiting for transfers between devices: 194 us -> 0 us
  blocking collectives: 71.3 us -> 0 us
  Pallas kernels: 0 us -> 40.3 us
  between operations: 13.9 us -> 0.75 us
  other arithmetic: 14.4 us -> 3.26 us
  matrix products: 19.4 us -> 9.25 us
  local copies, waits for them, and re-layouts: 8.22 us -> 2.88 us
    reduce_scatter x3 -> x0, waiting for transfers between devices: 194 us -> none  [the longest x1 71.5 us: local(): lax.psum_scatter(down_part, 'dp', scatter_dimension=0, tiled=True)]
    all_gather x2 -> x0, blocking collectives: 63.6 us -> none  [the longest x1 32 us: local(): scales = lax.all_gather(scale_own, 'dp', axis=1, tiled=True)]
    pallas_call x0 -> x1, Pallas kernels: none -> 40.3 us  [exchange(): pl.pallas_call(functools.partial(exchange_kernel, N, T, K, R), out_shape=...]
    dot_general x9 -> x1, matrix products: 19.4 us -> 9.25 us  [partial_norms(): shifted = jnp.einsum('sxh,shj->sxj', up, down, preferred_element_type=F32)]
    psum x2 -> x0, blocking collectives: 7.68 us -> none  [the longest x1 4.04 us: local(): rank_sum = lax.psum(rank_part, 'tensor')]
    convert_element_type x3 -> x1, other arithmetic: 10.3 us -> 3.26 us  [partial_norms(): merged = weight.astype(F32)[None] + shifted]
  transfers between devices with their start and end apart: 3 -> 0, of which waited for: 3 -> 0; matrix products, arithmetic and copies ran while one was open for 2% -> 0% of each run, Pallas kernels for 0% -> 0%
where the time goes in v1:
time: 56.6 us; the launch traced here: 56.4 us
  Pallas kernels  40.3 us (71%)
  matrix products  9.25 us (16%)
  other arithmetic  3.26 us (6%)
  local copies, waits for them, and re-layouts  2.88 us (5%)
  between operations  0.75 us (1%)
    pallas_call x1, Pallas kernels, exchange(): pl.pallas_call(functools.partial(exchange_kernel, N, T, K, R), out_shape=...  40.3 us
    dot_general x1, matrix products, partial_norms(): shifted = jnp.einsum('sxh,shj->sxj', up, down, preferred_element_type=F32)  9.25 us
    convert_element_type x1, other arithmetic, partial_norms(): merged = weight.astype(F32)[None] + shifted  3.26 us
    unnamed x15, local copies, waits for them, and re-layouts  2.08 us

profile of v1, /device:TPU:0, one launch (start us, length us, event | category | flops | bytes accessed | tf_op | source)
XLA Modules:
  0.0 56.4 jit_solution(8432089411381362035)
XLA Ops:
  0.6 0.0 copy-start
  0.6 0.0 copy-start.1
  0.7 0.8 %constant_dynamic-slice_fusion.mag_ref = f32[8,256]{1,0:T(8,128)S(1)} fusion(f32[8,512]{1,0:T(8,128)} %param.15, s32[]{:T(128)S(6)} %select_n.4), kind=kLoop, calls=%fused_computation.1 | loop fusion | bytes 16388 | tf_op jit(solution)/shard_map/dynamic_slice | solution.py:415
  1.5 0.1 copy-done
  1.5 3.3 %convert_element_type.3 = f32[512,4096]{1,0:T(8,128)S(1)} convert(bf16[512,4096]{1,0:T(8,128)(2,1)} %param.12) | non-fusion elementwise | flops 2097152 | bytes 12582912 | tf_op jit(solution)/shard_map/convert_element_type | solution.py:385
  4.8 0.0 copy-done.1
  4.8 0.0 copy-start.2
  4.8 0.0 copy-start.3
  4.8 0.0 copy-start.4
  4.9 0.0 copy-start.5
  4.9 9.2 %multiply_reduce_fusion.sq_ref = f32[8,512]{1,0:T(8,128)S(1)} fusion(bf16[8,512,16]{1,2,0:T(8,128)(2,1)S(1)} %copy-done, bf16[8,16,4096]{2,1,0:T(8,128)(2,1)S(1)} %copy-done.1, f32[512,4096]{1,0:T(8,128)S(1)} %convert_element_type.3), kind=kOutput, calls=%fused_computation | convolution fusion | flops 587198464 | bytes 9584640 | tf_op jit(solution)/shard_map/sxh,shj->sxj/dot_general | solution.py:384
  14.1 0.0 copy-done.2
  14.1 0.0 copy-done.3
  14.1 0.0 copy-done.4
  14.2 0.0 copy-done.5
  14.2 40.3 %shard_map.103 = (f32[128,256]{1,0:T(8,128)S(1)}, f32[8,256]{1,0:T(8,128)S(1)}, f32[16,4096]{1,0:T(8,128)S(1)}) custom-call(s32[2]{0:T(128)S(1)} %copy-done.5, bf16[128,4096]{1,0:T(8,128)(2,1)S(1)} %copy-done.2, bf16[128,4096]{1,0:T(8,128)(2,1)S(1)} %copy-done.3, bf16[128,4096]{1,0:T(8,128)(2,1)S(1)} %copy-done.4, bf16[128,4096]{1,0:T(8,128)(2,1)S(1)} %bitcast.9, ...), custom_call_target="tpu_custom_call" | custom-call | tf_op jit(solution)/shard_map/pallas_call | solution.py:357
  54.5 0.7 %copy.14 = f32[8,256,16]{1,2,0:T(8,128)} copy(f32[8,256,16]{1,2,0:T(8,128)S(1)} %bitcast.11) | data formatting | bytes 262144
  55.1 0.6 %copy.15 = f32[8,256]{1,0:T(8,128)} copy(f32[8,256]{1,0:T(8,128)S(1)} %get-tuple-element.13) | data formatting | bytes 16384
  55.7 0.7 %copy.16 = f32[16,4096]{1,0:T(8,128)} copy(f32[16,4096]{1,0:T(8,128)S(1)} %get-tuple-element.14) | data formatting | bytes 524288
  (1 shorter events, 0.0 us)
Async XLA Ops:
  0.6 0.9 %copy-start = (bf16[8,512,16]{1,2,0:T(8,128)(2,1)S(1)}, bf16[8,512,16]{1,2,0:T(8,128)(2,1)}, u32[]{:S(2)}) copy-start(bf16[8,512,16]{1,2,0:T(8,128)(2,1)} %param.14) | copy-start | bytes 393220
  0.6 4.2 %copy-start.1 = (bf16[8,16,4096]{2,1,0:T(8,128)(2,1)S(1)}, bf16[8,16,4096]{2,1,0:T(8,128)(2,1)}, u32[]{:S(2)}) copy-start(bf16[8,16,4096]{2,1,0:T(8,128)(2,1)} %param.13) | copy-start | bytes 3145732
  4.8 9.3 %copy-start.2 = (bf16[128,4096]{1,0:T(8,128)(2,1)S(1)}, bf16[128,4096]{1,0:T(8,128)(2,1)}, u32[]{:S(2)}) copy-start(bf16[128,4096]{1,0:T(8,128)(2,1)} %x_ref.1) | copy-start | bytes 3145732
  4.8 9.3 %copy-start.3 = (bf16[128,4096]{1,0:T(8,128)(2,1)S(1)}, bf16[128,4096]{1,0:T(8,128)(2,1)}, u32[]{:S(2)}) copy-start(bf16[128,4096]{1,0:T(8,128)(2,1)} %g_ref.1) | copy-start | bytes 3145732
  4.8 9.3 %copy-start.4 = (bf16[128,4096]{1,0:T(8,128)(2,1)S(1)}, bf16[128,4096]{1,0:T(8,128)(2,1)}, u32[]{:S(2)}) copy-start(bf16[128,4096]{1,0:T(8,128)(2,1)} %f_ref.1) | copy-start | bytes 3145732
  4.9 9.3 %copy-start.5 = (s32[2]{0:T(128)S(1)}, s32[2]{0:T(128)}, u32[]{:S(2)}) copy-start(s32[2]{0:T(128)} %ten_ref.1) | copy-start | bytes 28

commit v2 on v1

--- a/solution.py
+++ b/solution.py
@@ -99,6 +99,7 @@
 
 
 F32 = jnp.float32
+CHUNK = 512
 BF16 = jnp.bfloat16
 NT = (((1,), (1,)), ((), ()))
 
@@ -109,11 +110,12 @@
 
 def exchange_kernel(
     N, T, K, R,
-    ten_ref, x_ref, g_ref, f_ref, down_ref, up_ref, mag_ref, sq_ref,
+    ten_ref, x_hbm, g_hbm, f_hbm, down_hbm, w_hbm, up_ref, mag_ref,
     up_out, mag_out, down_out,
+    x_ref, g_ref, f_ref, down_ref, w_ref, um, sq_acc, sq_send,
     g_buf, aux_send, aux_buf, sq_buf, rp_send, rp_buf, ra_buf, up_acc, z_acc, fg_acc,
     back_send, back_buf, tile_send, tile_buf, part_send, part_buf,
-    g_ss, g_rs, aux_ss, aux_rs, pair_ss, pair_rs, ra_ss, ra_rs,
+    load, g_ss, g_rs, aux_ss, aux_rs, pair_ss, pair_rs, ra_ss, ra_rs, sq_rs,
     back_ss, back_rs, tile_ss, tile_rs, part_ss, part_rs,
 ):
     me = lax.axis_index("dp")
@@ -122,8 +124,21 @@
     tok = x_ref.shape[0]
     half = tok // 2
     width = x_ref.shape[1] // N
-    C = up_ref.shape[1]
+    C = mag_ref.shape[1] // T
     KR = K * R
+    group = lax.axis_index("groups")
+
+    loads = [
+        pltpu.make_async_copy(down_hbm, down_ref, load.at[0]),
+        pltpu.make_async_copy(x_hbm, x_ref, load.at[1]),
+        pltpu.make_async_copy(
+            w_hbm.at[pl.ds(pl.multiple_of(group * C, C), C), :], w_ref, load.at[2]
+        ),
+        pltpu.make_async_copy(g_hbm, g_ref, load.at[3]),
+        pltpu.make_async_copy(f_hbm, f_ref, load.at[4]),
+    ]
+    for one in loads:
+        one.start()
 
     def copy(src, dst, ss, rs, dp, tensor):
         return pltpu.make_async_remote_copy(
@@ -141,7 +156,12 @@
                 barrier, inc=1, device_id={"dp": peer(off), "tensor": t},
                 device_id_type=pl.DeviceIdType.MESH,
             )
-    pl.semaphore_wait(barrier, 2 * N - 1)
+    for t in range(T):
+        pl.semaphore_signal(
+            barrier, inc=1, device_id={"groups": 1 - group, "dp": me, "tensor": t},
+            device_id_type=pl.DeviceIdType.MESH,
+        )
+    pl.semaphore_wait(barrier, 2 * N - 1 + T)
 
     def cols(d):
         return pl.ds(pl.multiple_of((d * T + core) * C, C), C)
@@ -150,16 +170,10 @@
         return pl.ds(pl.multiple_of(d * width, width), width)
 
     def g_copy(d):
-        return copy(g_ref.at[:, cols(d)], g_buf.at[me], g_ss.at[d], g_rs.at[me], d, core)
+        return copy(g_hbm.at[:, cols(d)], g_buf.at[me], g_ss.at[d], g_rs.at[me], d, core)
 
     def aux_copy(d):
         return copy(aux_send.at[d], aux_buf.at[me], aux_ss.at[d], aux_rs.at[me], d, core)
-
-    sq_copy = copy(
-        sq_ref.at[:, pl.ds(pl.multiple_of(other * C, C), C)], sq_buf,
-        pair_ss.at[0], pair_rs.at[0], me, other,
-    )
-    sq_copy.start()
 
     def start_g(off, _):
         g_copy(peer(off)).start()
@@ -172,6 +186,8 @@
     own_ten = jnp.where(lane_tok < half, ten0, ten1)
     own_mask = (iota((KR, tok), 0) // R) == own_ten
 
+    loads[0].wait()
+    loads[1].wait()
     proj = lax.dot_general(down_ref[...], x_ref[...], NT, preferred_element_type=F32)
     rp_send[...] = jnp.sum(jnp.where(own_mask, proj, 0.0).reshape(K, R, tok), axis=0)
     rp_copy = copy(rp_send, rp_buf, pair_ss.at[1], pair_rs.at[1], me, other)
@@ -186,6 +202,9 @@
     ids = jnp.where(rows == 2, ids0, jnp.where(rows == 3, ids1, jnp.where(rows == 4, tok_ids, slot_ids)))
     ids = jnp.where((rows >= 2) & (rows <= 5), ids, 0).astype(F32)
 
+    loads[3].wait()
+    loads[4].wait()
+
     def make_aux(off, _):
         d = peer(off)
         prod = g_ref[:, cols(d)].astype(F32) * f_ref[:, cols(d)].astype(F32)
@@ -216,10 +235,59 @@
         return 0
     lax.fori_loop(1, N, start_ra, 0)
 
-    sq_copy.wait_recv()
-    norm = jnp.sqrt(sq_ref[:, pl.ds(pl.multiple_of(core * C, C), C)] + sq_buf[...])
-    scale = mag_ref[...] / norm
-    up = up_ref[...]
+    loads[2].wait()
+    ut = up_ref[:, pl.ds(pl.multiple_of(group * C, C), C)].astype(F32).T
+    for k in range(K):
+        um[k] = jnp.where(iota((C, KR), 1) // R == k, ut, 0.0).astype(BF16)
+    sq_acc[...] = jnp.zeros_like(sq_acc)
+
+    def norm_chunk(c, _):
+        at = pl.ds(pl.multiple_of(c * CHUNK, CHUNK), CHUNK)
+        w = w_ref[:, at].astype(F32)
+        d = down_ref[:, at]
+        for k in range(K):
+            m = w + jnp.dot(um[k], d, preferred_element_type=F32)
+            m = m * m
+            total = m[:, :128]
+            for b in range(128, CHUNK, 128):
+                total = total + m[:, b:b + 128]
+            sq_acc[k] += total
+        return 0
+    lax.fori_loop(0, w_ref.shape[1] // CHUNK, norm_chunk, 0)
+    square = jnp.zeros((C, 128), F32)
+    for k in range(K):
+        square = jnp.where(iota((C, 128), 1) == k, jnp.sum(sq_acc[k], axis=1, keepdims=True), square)
+    sq_send[...] = square.T[:K]
+
+    def sq_copy(gr, i):
+        return pltpu.make_async_remote_copy(
+            src_ref=sq_send, dst_ref=sq_buf.at[core], send_sem=pair_ss.at[i],
+            recv_sem=sq_rs.at[core], device_id={"groups": gr, "dp": me, "tensor": group},
+            device_id_type=pl.DeviceIdType.MESH,
+        )
+    sq_copy(1 - group, 0).start()
+
+    @pl.when(core == group)
+    def _():
+        sq_buf[core] = sq_send[...]
+
+    @pl.when(core != group)
+    def _():
+        sq_copy(group, 2).start()
+
+    def wait_sq(t):
+        copy(sq_send, sq_buf.at[t], pair_ss.at[0], sq_rs.at[t], me, other).wait_recv()
+    wait_sq(other)
+
+    @pl.when(core != group)
+    def _():
+        wait_sq(core)
+        sq_copy(group, 2).wait_send()
+    sq_copy(1 - group, 0).wait_send()
+    own = pl.ds(pl.multiple_of(core * C, C), C)
+    norm = jnp.sqrt(sq_buf[0] + sq_buf[1])
+    scale = mag_ref[:, own] / norm
+    up = up_ref[:, own]
 
     up_acc[...] = jnp.zeros_like(up_acc)
     z_acc[...] = jnp.zeros_like(z_acc)
@@ -331,7 +399,6 @@
         back_copy(d, other).wait_send()
         tile_copy(d).wait_send()
         return 0
-    sq_copy.wait_send()
     rp_copy.wait_send()
     back_copy(me, other).wait_send()
     lax.fori_loop(1, N, wait_sends, 0)
@@ -347,13 +414,15 @@
     lax.fori_loop(1, N, finish, 0)
 
 
-def exchange(ten, x, g, f, down, up, mag, sq, N, T, K, R):
+def exchange(ten, x, g, f, down, w, up, mag, N, T, K, R):
     tok, I = x.shape
-    C = up.shape[1]
+    O = g.shape[1]
+    C = up.shape[1] // T
     width = I // N
     vm = pltpu.VMEM
     dma = pltpu.SemaphoreType.DMA
     spec = pl.BlockSpec(memory_space=pltpu.VMEM)
+    hbm = pl.BlockSpec(memory_space=pl.ANY)
     return pl.pallas_call(
         functools.partial(exchange_kernel, N, T, K, R),
         out_shape=(
@@ -361,29 +430,26 @@
             jax.ShapeDtypeStruct((K, C), F32),
             jax.ShapeDtypeStruct((R, I), F32),
         ),
-        in_specs=[pl.BlockSpec(memory_space=pltpu.SMEM)] + [spec] * 7,
+        in_specs=[pl.BlockSpec(memory_space=pltpu.SMEM)] + [hbm] * 5 + [spec] * 2,
         out_specs=(spec, spec, spec),
         scratch_shapes=[
-            vm((N, tok, C), BF16), vm((N, 8, C), F32), vm((N, 8, C), F32), vm((K, C), F32),
+            vm((tok, I), BF16), vm((tok, O), BF16), vm((tok, O), BF16), vm((K * R, I), BF16),
+            vm((C, I), BF16), vm((K, C, K * R), BF16), vm((K, C, 128), F32), vm((K, C), F32),
+            vm((N, tok, C), BF16), vm((N, 8, C), F32), vm((N, 8, C), F32), vm((T, K, C), F32),
             vm((R, tok), F32), vm((R, tok), F32), vm((N, R, tok), BF16),
             vm((K * R, C), F32), vm((K * R, C), F32), vm((K, C), F32),
             vm((N, R, tok), F32), vm((N * T, R, tok), F32),
             vm((N, 2 * R, width), BF16), vm((N, 2 * R, width), BF16),
             vm((N, R, width), BF16), vm((N, R, width), BF16),
-            dma((N,)), dma((N,)), dma((N,)), dma((N,)), dma((2,)), dma((2,)),
-            dma((N,)), dma((N,)), dma((N * T,)), dma((N * T,)),
+            dma((5,)),
+            dma((N,)), dma((N,)), dma((N,)), dma((N,)), dma((3,)), dma((3,)),
+            dma((N,)), dma((N,)), dma((T,)), dma((N * T,)), dma((N * T,)),
             dma((N,)), dma((N,)), dma((N,)), dma((N,)),
         ],
         compiler_params=pltpu.CompilerParams(
-            collective_id=0, has_side_effects=True, vmem_limit_bytes=40 * 1024 * 1024
+            collective_id=0, has_side_effects=True, vmem_limit_bytes=56 * 1024 * 1024
         ),
-    )(ten, x, g, f, down, up, mag, sq)
-
-
-def partial_norms(weight, down, up):
-    shifted = jnp.einsum("sxh,shj->sxj", up, down, preferred_element_type=F32)
-    merged = weight.astype(F32)[None] + shifted
-    return jnp.sum(merged * merged, axis=2)
+    )(ten, x, g, f, down, w, up, mag)
 
 
 def local(
@@ -402,20 +468,17 @@
     own = frozen_weight.shape[0]
     C = own // T
     if not (
-        N == K and T == 2 and R == 16 and K == 8 and C == N * 2 * R
-        and inputs.shape[0] == 128 and tenant_of_tile.shape[0] == 2 and I % (128 * N) == 0
+        N == K and T == 2 and lax.axis_size("groups") == 2 and R == 16 and K == 8 and C == N * 2 * R
+        and inputs.shape[0] == 128 and tenant_of_tile.shape[0] == 2 and I % CHUNK == 0 and I % (128 * N) == 0
     ):
         return plain(
             inputs, output_gradient, frozen_output, tenant_of_tile,
             frozen_weight, adapter_down, adapter_up, magnitude,
         )
-    sq = partial_norms(frozen_weight, adapter_down, adapter_up)
-    at = lax.axis_index("tensor") * C
-    up = jnp.transpose(lax.dynamic_slice_in_dim(adapter_up, at, C, 1), (0, 2, 1)).reshape(K * R, C)
-    mag = lax.dynamic_slice_in_dim(magnitude, at, C, 1)
+    up = jnp.transpose(adapter_up, (0, 2, 1)).reshape(K * R, own)
     up_sum, grad_mag, grad_down = exchange(
         tenant_of_tile, inputs, output_gradient, frozen_output,
-        adapter_down.reshape(K * R, I), up, mag, sq, N, T, K, R,
+        adapter_down.reshape(K * R, I), frozen_weight, up, magnitude, N, T, K, R,
     )
     grad_up = jnp.transpose(up_sum.reshape(K, R, C), (0, 2, 1))
     return (grad_up, grad_mag, grad_down)

time: 56.6 us -> 47.1 us (0.83)
  matrix products: 9.25 us -> 0 us
  other arithmetic: 3.26 us -> 0 us
  local copies, waits for them, and re-layouts: 2.88 us -> 4.53 us
  Pallas kernels: 40.3 us -> 41.7 us
    dot_general x1 -> x0, matrix products: 9.25 us -> none  [partial_norms(): shifted = jnp.einsum('sxh,shj->sxj', up, down, preferred_element_type=F32)]
    convert_element_type x1 -> x0, other arithmetic: 3.26 us -> none  [partial_norms(): merged = weight.astype(F32)[None] + shifted]
    unnamed x15 -> x3, local copies, waits for them, and re-layouts: 2.08 us -> 4.53 us
    pallas_call x1, Pallas kernels: 40.3 us -> 41.7 us  [exchange(): pl.pallas_call(functools.partial(exchange_kernel, N, T, K, R), out_shape=...]
    dynamic_slice x2 -> x0, local copies, waits for them, and re-layouts: 0.8 us -> none  [the longest x1 0.8 us: local(): mag = lax.dynamic_slice_in_dim(magnitude, at, C, 1)]
where the time goes in v2:
time: 47.1 us; the launch traced here: 46.9 us
  Pallas kernels  41.7 us (89%)
  local copies, waits for them, and re-layouts  4.53 us (10%)
  between operations  0.64 us (1%)
    pallas_call x1, Pallas kernels, exchange(): pl.pallas_call(functools.partial(exchange_kernel, N, T, K, R), out_shape=...  41.7 us
    unnamed x3, local copies, waits for them, and re-layouts  4.53 us

profile of v2, /device:TPU:0, one launch (start us, length us, event | category | flops | bytes accessed | tf_op | source)
XLA Modules:
  0.0 46.9 jit_solution(6036358960188185555)
XLA Ops:
  0.6 41.7 %shard_map.103 = (f32[128,256]{1,0:T(8,128)}, f32[8,256]{1,0:T(8,128)}, f32[16,4096]{1,0:T(8,128)}) custom-call(s32[2]{0:T(128)} %ten_ref.1, bf16[128,4096]{1,0:T(8,128)(2,1)} %x_hbm.1, bf16[128,4096]{1,0:T(8,128)(2,1)} %g_hbm.1, bf16[128,4096]{1,0:T(8,128)(2,1)} %f_hbm.1, bf16[128,4096]{1,0:T(8,128)(2,1)} %bitcast.7, bf16[512,4096]{1,0:T(8,128)(2,1)} %w_hbm.1, ...), custom_call_target="tpu_custom_call" | custom-call | tf_op jit(solution)/shard_map/pallas_call | solution.py:426
  42.3 1.6 %copy.14 = f32[8,256,16]{1,2,0:T(8,128)} copy(f32[8,256,16]{1,2,0:T(8,128)} %bitcast.9) | data formatting | bytes 262144
  43.9 1.3 %copy.15 = f32[8,256]{1,0:T(8,128)} copy(f32[8,256]{1,0:T(8,128)} %get-tuple-element.13) | data formatting | bytes 16384
  45.2 1.7 %copy.16 = f32[16,4096]{1,0:T(8,128)} copy(f32[16,4096]{1,0:T(8,128)} %get-tuple-element.14) | data formatting | bytes 524288

commit v3 on v2

--- a/solution.py
+++ b/solution.py
@@ -338,10 +338,14 @@
         return 0
     lax.fori_loop(1, N, remote_block, 0)
 
-    up_sum = up_acc[...]
-    up_out[...] = up_sum
     mixed = jnp.sum((up.astype(F32) * z_acc[...]).reshape(K, R, C), axis=1)
-    mag_out[...] = (fg_acc[...] + mixed) / norm
+    fg_acc[...] = (fg_acc[...] + mixed) / norm
+    writes = [
+        pltpu.make_async_copy(up_acc, up_out, load.at[0]),
+        pltpu.make_async_copy(fg_acc, mag_out, load.at[1]),
+    ]
+    for one in writes:
+        one.start()
 
     def wait_back(s, t):
         i = s * T + t
@@ -412,6 +416,8 @@
         part_copy(s).wait_send()
         return 0
     lax.fori_loop(1, N, finish, 0)
+    for one in writes:
+        one.wait()
 
 
 def exchange(ten, x, g, f, down, w, up, mag, N, T, K, R):
@@ -431,7 +437,7 @@
             jax.ShapeDtypeStruct((R, I), F32),
         ),
         in_specs=[pl.BlockSpec(memory_space=pltpu.SMEM)] + [hbm] * 5 + [spec] * 2,
-        out_specs=(spec, spec, spec),
+        out_specs=(hbm, hbm, spec),
         scratch_shapes=[
             vm((tok, I), BF16), vm((tok, O), BF16), vm((tok, O), BF16), vm((K * R, I), BF16),
             vm((C, I), BF16), vm((K, C, K * R), BF16), vm((K, C, 128), F32), vm((K, C), F32),

time: 47.1 us -> 47.1 us (level)
  no operation moved by 1% of the time
where the time goes in v3:
time: 47.1 us; the launch traced here: 46.8 us
  Pallas kernels  41.6 us (88%)
  local copies, waits for them, and re-layouts  4.53 us (10%)
  between operations  0.64 us (1%)
    pallas_call x1, Pallas kernels, exchange(): pl.pallas_call(functools.partial(exchange_kernel, N, T, K, R), out_shape=...  41.6 us
    unnamed x3, local copies, waits for them, and re-layouts  4.53 us

profile of v3, /device:TPU:0, one launch (start us, length us, event | category | flops | bytes accessed | tf_op | source)
XLA Modules:
  0.0 46.8 jit_solution(1944175351051618128)
XLA Ops:
  0.6 41.6 %shard_map.103 = (f32[128,256]{1,0:T(8,128)}, f32[8,256]{1,0:T(8,128)}, f32[16,4096]{1,0:T(8,128)}) custom-call(s32[2]{0:T(128)} %ten_ref.1, bf16[128,4096]{1,0:T(8,128)(2,1)} %x_hbm.1, bf16[128,4096]{1,0:T(8,128)(2,1)} %g_hbm.1, bf16[128,4096]{1,0:T(8,128)(2,1)} %f_hbm.1, bf16[128,4096]{1,0:T(8,128)(2,1)} %bitcast.7, bf16[512,4096]{1,0:T(8,128)(2,1)} %w_hbm.1, ...), custom_call_target="tpu_custom_call" | custom-call | tf_op jit(solution)/shard_map/pallas_call | solution.py:432
  42.3 1.6 %copy.14 = f32[8,256,16]{1,2,0:T(8,128)} copy(f32[8,256,16]{1,2,0:T(8,128)} %bitcast.9) | data formatting | bytes 262144
  43.9 1.3 %copy.15 = f32[8,256]{1,0:T(8,128)} copy(f32[8,256]{1,0:T(8,128)} %get-tuple-element.13) | data formatting | bytes 16384
  45.2 1.7 %copy.16 = f32[16,4096]{1,0:T(8,128)} copy(f32[16,4096]{1,0:T(8,128)} %get-tuple-element.14) | data formatting | bytes 524288
